TPU v7x, 256 devices: a whole 4x4x8 slice. The times are simulated.
256 devices in a mesh: tm: 16 (over z, y_lo), mesh: 16 (over y_hi, x, core).
Axes of the slice: x: 4, y: 4 (y_hi: 2, y_lo: 2; y = y_hi * 2 + y_lo), z: 8, core: 2. Of those that a mesh axis runs over, the one named last changes fastest.
Arguments:
- adjoint: bfloat16 [2, 16, 128, 320, 128], P(None, 'tm', 'mesh'), may hold values from -6 to 6
- source: bfloat16 [2, 16, 128, 320, 128], P(None, 'tm', 'mesh'), may hold values from -6 to 6
- block_inverse: bfloat16 [2, 16, 128, 320, 320], P(None, 'tm', 'mesh'), may hold values from -1 to 1
- face_partials: bfloat16 [2, 16, 128, 6, 80, 320], P(None, 'tm', 'mesh'), may hold values from -0.625 to 0.625
- mass: float32 [128, 320], P('mesh'), may hold values from 0.4 to 2.5
Outputs:
- updated: bfloat16 [2, 16, 128, 320, 128], P(None, 'tm', 'mesh')
All inputs are finite; a program needn't handle non-finite values.
Results may differ from a plain program's by a relative error of at most 0.017.
Values may be sent and summed in bfloat16 or wider, within the bound.
No kernel may reach another device: no remote copies, remote signals or barrier semaphores. Data moves between devices by JAX's collectives and lax.ppermute only.
A program may use at most 128 MiB of HBM per device.

v0:
```python
import math

import jax
import jax.numpy as jnp
from jax import lax
from jax.sharding import PartitionSpec as P

VARS = 5
P1 = 4
EY = 4
EZ = 2
LAY_DEV = 1
RHS = 128
FACE = 80


OMEGA_TIME = 0.25


def from_behind(value, axis, steps):
    count = lax.axis_size(axis)
    first, last = (max(0, -steps), min(count, count - steps))
    return lax.ppermute(value, axis, [(source, source + steps) for source in range(first, last)])


def time_weights(source_index, target_index, period):
    offset = source_index - target_index
    parity = jnp.mod(offset, 2)
    signs = (1 - 2 * parity).astype(jnp.float32)
    angle = math.pi / period * offset.astype(jnp.float32)
    is_self = offset == 0
    sine = jnp.where(is_self, jnp.ones_like(angle), jnp.sin(angle))
    return jnp.where(is_self, jnp.zeros_like(angle), 0.5 * signs * jnp.cos(angle) / sine)


def split_mix(pattern, weights, piece):
    upper_part = weights.astype(jnp.bfloat16)
    lower_part = (weights - upper_part.astype(jnp.float32)).astype(jnp.bfloat16)
    first = jnp.einsum(pattern, upper_part, piece, preferred_element_type=jnp.float32)
    second = jnp.einsum(pattern, lower_part, piece, preferred_element_type=jnp.float32)
    return first + second


def neighbour_traces(field, lower_rim, upper_rim):
    x_low = field[:, :, :, :, :, -1]
    x_high = field[:, :, :, :, :, 0]
    minus_x = jnp.concatenate([lower_rim[:, None], x_low[:, :-1]], axis=1)
    plus_x = jnp.concatenate([x_high[:, 1:], upper_rim[:, None]], axis=1)
    minus_y = jnp.roll(field[:, :, :, :, :, :, -1], 1, axis=2)
    plus_y = jnp.roll(field[:, :, :, :, :, :, 0], -1, axis=2)
    z_low = field[:, :, :, :, :, :, :, -1]
    z_high = field[:, :, :, :, :, :, :, 0]
    blank = jnp.zeros_like(z_low[:, :, :, :1])
    minus_z = jnp.concatenate([blank, z_low[:, :, :, :-1]], axis=3)
    plus_z = jnp.concatenate([z_high[:, :, :, 1:], blank], axis=3)
    return jnp.stack([minus_x, plus_x, minus_y, plus_y, minus_z, plus_z], axis=4)


def per_device(adjoint, source, block_inverse, face_partials, mass):
    elements = adjoint.shape[2]
    columns = adjoint.shape[4]
    count = lax.axis_size("tm")
    period = 2 * count
    member = lax.axis_index("tm")
    grid = adjoint[:, 0].reshape(2, LAY_DEV, EY, EZ, VARS, P1, P1, P1, RHS)
    lower_rim = from_behind(grid[:, -1, :, :, :, -1], "mesh", 1)
    upper_rim = from_behind(grid[:, 0, :, :, :, 0], "mesh", -1)
    traces = neighbour_traces(grid, lower_rim, upper_rim).reshape(2, elements, 6, FACE, columns)
    coupling = jnp.einsum(
        "hefkq,hefkr->heqr", face_partials[:, 0], traces, preferred_element_type=jnp.float32
    )
    halves = jnp.arange(2, dtype=jnp.int32)
    target = halves * count + member
    piece = lax.all_gather(adjoint, "tm", axis=1, tiled=True)
    width = piece.shape[1]
    anchor = halves[:, None] * count + jnp.arange(width, dtype=jnp.int32)[None, :]
    weights = time_weights(anchor[:, :, None], target[None, None, :], period)
    spectral = split_mix("gjh,gjeqr->heqr", weights, piece).astype(jnp.bfloat16)
    residual = (
        source[:, 0].astype(jnp.float32)
        - coupling
        - OMEGA_TIME * mass[None, :, :, None] * spectral.astype(jnp.float32)
    ).astype(jnp.bfloat16)
    updated = jnp.einsum(
        "heqp,hepr->heqr", block_inverse[:, 0], residual, preferred_element_type=jnp.float32
    ).astype(jnp.bfloat16)
    return updated[:, None]


def solution(mesh):
    return jax.shard_map(
        per_device,
        mesh=mesh,
        in_specs=(
            P(None, "tm", "mesh", None, None),
            P(None, "tm", "mesh", None, None),
            P(None, "tm", "mesh", None, None),
            P(None, "tm", "mesh", None, None, None),
            P("mesh", None),
        ),
        out_specs=P(None, "tm", "mesh", None, None),
        check_vma=False,
    )
```

profile of v0, /device:TPU:6, one launch (start us, length us, event | category | flops | bytes accessed | tf_op | source)
XLA Modules:
  0.0 498.5 jit_solution(17586889905960981103)
XLA Ops:
  6.5 0.0 copy-start
  6.5 0.0 all-gather.2.cloned.1.call-start
  6.5 0.7 all-gather.2.cloned.1.call-update
  7.3 1.3 slice_bitcast_fusion.2
  8.6 1.9 collective-permute-start
  10.5 3.6 collective-permute-start.1
  14.2 0.0 copy-done
  14.2 0.2 slice_bitcast_fusion
  14.4 0.1 slice.56
  14.6 0.1 slice.58
  14.7 1.3 fusion.54
  16.0 0.0 copy-start.3
  16.0 0.2 copy_bitcast_fusion
  16.3 0.1 slice.61
  16.3 0.1 slice.63
  16.4 0.1 concatenate.17
  16.5 0.1 concatenate.18
  16.6 0.2 pad_maximum_fusion
  16.9 0.2 pad_maximum_fusion.1
  17.1 0.0 copy-done.3
  17.1 0.1 iota_add_fusion
  17.2 0.0 collective-permute-done
  17.2 1.5 collective-permute-done.1
  19.0 4.6 fusion.4
  23.6 423.8 %all-gather.2.cloned.1.call-done = bf16[2,16,8,320,128]{4,3,2,1,0:T(8,128)(2,1)} async-done(((bf16[2,1,8,320,128]{4,3,2,1,0:T(8,128)(2,1)}), bf16[2,16,8,320,128]{4,3,2,1,0:T(8,128)(2,1)}) %all-gather.2.cloned.1.call-update) | async-done | bytes 20971536 | tf_op jit(solution)/shard_map/all_gather | solution.py:74
  447.3 20.6 %fusion = f32[2,8,320,128,1]{3,0,4,2,1:T(2,128)S(1)} fusion(bf16[2,16,8,320,128]{4,3,2,1,0:T(8,128)(2,1)} %all-gather.2.cloned.1.call-done, s32[2]{0:T(128)S(1)} %broadcast_add_fusion, s32[2,16]{1,0:T(2,128)S(1)} %iota_add_fusion), kind=kOutput, calls=%fused_computation | convolution fusion | flops 41944768 | bytes 23593096 | tf_op jit(solution)/shard_map/gjh,gjeqr->heqr/dot_general | solution.py:40
  468.0 0.0 copy-start.1
  468.0 0.0 copy-start.2
  468.0 21.0 %fusion.2 = f32[2,8,320,128,1]{3,0,4,2,1:T(2,128)S(1)} fusion(bf16[2,16,8,320,128]{4,3,2,1,0:T(8,128)(2,1)} %all-gather.2.cloned.1.call-done, s32[2]{0:T(128)S(1)} %broadcast_add_fusion, s32[2,16]{1,0:T(2,128)S(1)} %iota_add_fusion), kind=kOutput, calls=%fused_computation.2 | convolution fusion | flops 41944576 | bytes 23593096 | tf_op jit(solution)/shard_map/gjh,gjeqr->heqr/dot_general | solution.py:39
  489.0 0.0 copy-done.1
  489.0 0.0 copy-done.2
  489.0 2.7 fusion.15
  (11 shorter events, 0.3 us)
Async XLA Ops:
  6.5 7.6 %copy-start = (bf16[2,1,8,320,128]{4,3,2,1,0:T(8,128)(2,1)S(1)}, bf16[2,1,8,320,128]{4,3,2,1,0:T(8,128)(2,1)}, u32[]{:S(2)}) copy-start(bf16[2,1,8,320,128]{4,3,2,1,0:T(8,128)(2,1)} %param.5) | copy-start | bytes 3932164
  6.5 440.8 %all-gather.2.cloned.1.call-start = ((), (), s32[]{:S(2)}) async-start(), calls=%async_computation | async-start | bytes 22282240 | tf_op jit(solution)/shard_map/all_gather | solution.py:74
  8.6 8.6 %collective-permute-start = (bf16[2,4,2,5,4,4,128]{6,5,4,3,2,1,0:T(4,128)(2,1)S(1)}, bf16[2,4,2,5,4,4,128]{6,5,4,3,2,1,0:T(4,128)(2,1)S(1)}, u32[]{:S(2)}, u32[]{:S(2)}) collective-permute-start(bf16[2,4,2,5,4,4,128]{6,5,4,3,2,1,0:T(4,128)(2,1)S(1)} %get-tuple-element.10), channel_id=1, source_target_pairs={{0,1},{1,2},{2,3},{3,4},{4,5},{5,6},{6,7},{7,8},{8,9},{9,10},{10,1... | collective-permute-start | bytes 983048 | tf_op jit(solution)/shard_map/ppermute | solution.py:23
  10.5 8.2 %collective-permute-start.1 = (bf16[2,4,2,5,4,4,128]{6,5,4,3,2,1,0:T(4,128)(2,1)S(1)}, bf16[2,4,2,5,4,4,128]{6,5,4,3,2,1,0:T(4,128)(2,1)S(1)}, u32[]{:S(2)}, u32[]{:S(2)}) collective-permute-start(bf16[2,4,2,5,4,4,128]{6,5,4,3,2,1,0:T(4,128)(2,1)S(1)} %get-tuple-element.9), channel_id=1, source_target_pairs={{1,0},{2,1},{3,2},{4,3},{5,4},{6,5},{7,6},{8,7},{9,8},{10,9},{11,1... | collective-permute-start | bytes 983048 | tf_op jit(solution)/shard_map/ppermute | solution.py:23
  16.0 1.1 copy-start.3
  468.0 21.0 %copy-start.1 = (bf16[2,1,8,320,320]{4,3,2,1,0:T(8,128)(2,1)S(1)}, bf16[2,1,8,320,320]{4,3,2,1,0:T(8,128)(2,1)}, u32[]{:S(2)}) copy-start(bf16[2,1,8,320,320]{4,3,2,1,0:T(8,128)(2,1)} %param.7) | copy-start | bytes 9830404
  468.0 21.0 %copy-start.2 = (bf16[2,1,8,320,128]{4,3,2,1,0:T(8,128)(2,1)S(1)}, bf16[2,1,8,320,128]{4,3,2,1,0:T(8,128)(2,1)}, u32[]{:S(2)}) copy-start(bf16[2,1,8,320,128]{4,3,2,1,0:T(8,128)(2,1)} %param.6) | copy-start | bytes 3932164
Sparse Core Ops, SparseCore 0:
  9.2 438.1 all-gather.1
where the time goes:
time: 504 us; the launch traced here: 499 us
  waiting for transfers between devices  426 us (85%)
  matrix products  48.9 us (10%)
  between operations  13.6 us (3%)
  starting transfers between devices  5.56 us (1%)
    all_gather x1, waiting for transfers between devices, per_device(): piece = lax.all_gather(adjoint, 'tm', axis=1, tiled=True)  424 us
    dot_general x1, matrix products, split_mix(): jnp.einsum(pattern, upper_part, piece, preferred_element_type=jnp.float32)  21 us
    dot_general x1, matrix products, split_mix(): jnp.einsum(pattern, lower_part, piece, preferred_element_type=jnp.float32)  20.6 us
  transfers between devices with their start and end apart: 3, of which 2 were waited for; matrix products, arithmetic and copies ran while one was open for 2% of the time, Pallas kernels for 0%

commit v1 on v0

v1 whole, which is shorter than its diff:
```python
import math

import jax
import jax.numpy as jnp
import numpy as np
from jax import lax
from jax.experimental import pallas as pl
from jax.experimental.pallas import tpu as pltpu
from jax.sharding import PartitionSpec as P

VARS = 5
P1 = 4
EY = 4
EZ = 2
LAY_DEV = 1
RHS = 128
BLOCK = 320
FACE = 80
OMEGA_TIME = 0.25

RING = 8
TIMES = 32
HALF = 16
ROLES = 4
ORDER = (1, 0, 3, 2)
OWN, OTHER = 0, 1
FAR = 3
AHEAD = 2
PIECE = (2, BLOCK, RHS)


def spectral_weight(offset):
    offset = offset % TIMES
    if offset in (0, HALF):
        return 0.0
    return 0.5 * (-1) ** offset / math.tan(math.pi * offset / TIMES)


def weight_slot(source_step, target_step, source_column, target_column):
    row = (target_step + AHEAD) * (2 * FAR + 1) + source_step + FAR
    return 2 * (4 * row + 2 * source_column + target_column)


def weight_table():
    table = np.zeros((HALF, 8 * (2 * AHEAD + 1) * (2 * FAR + 1)), np.float32)
    for member in range(HALF):
        z, y = divmod(member, 2)
        for target_step in range(-AHEAD, AHEAD + 1):
            for source_step in range(-FAR, FAR + 1):
                for source_column in (OWN, OTHER):
                    for target_column in (OWN, OTHER):
                        source = (z + source_step) % RING * 2 + (y ^ source_column)
                        target = (z + target_step) % RING * 2 + (y ^ target_column)
                        near = spectral_weight(source - target)
                        far = spectral_weight(source - target + HALF)
                        slot = weight_slot(source_step, target_step, source_column, target_column)
                        table[member, slot] = 0.5 * (near + far)
                        table[member, slot + 1] = 0.5 * (near - far)
    return table


def element_table():
    table = np.zeros((HALF, 2 * ROLES), np.int32)
    for member in range(HALF):
        z, y = divmod(member, 2)
        for place, role in enumerate(ORDER):
            table[member, place] = y * ROLES + (z - role) % ROLES
            table[member, ROLES + place] = (1 - y) * ROLES + (z - role) % ROLES
    return table


def column_pairs(step, swap):
    return [
        (z * 2 + y, (z + step) % RING * 2 + (y ^ swap)) for z in range(RING) for y in range(2)
    ]


def send(value, step, swap=0):
    return lax.ppermute(value, "tm", column_pairs(step, swap))


def combine(weights, groups, dtypes, rows=80):
    operands, operand_of = [], {}
    for sources, _ in groups:
        for array, place, _, _ in sources:
            if (id(array), place) not in operand_of:
                operand_of[id(array), place] = len(operands)
                operands.append((array, place))
    slots = [0] * len(dtypes)
    stores = []
    for _, targets in groups:
        placed = []
        for step, column, output in targets:
            placed.append((step, column, output, slots[output]))
            slots[output] += 1
        stores.append(placed)

    def kernel(weights_ref, *refs):
        inputs, outputs = refs[: len(operands)], refs[len(operands):]
        for (sources, _), targets in zip(groups, stores):
            sums = [None] * len(targets)
            for array, place, source_step, source_column in sources:
                ref = inputs[operand_of[id(array), place]]
                first = ref[0, 0].astype(jnp.float32)
                second = ref[0, 1].astype(jnp.float32)
                plus, minus = first + second, first - second
                for index, (step, column, _, _) in enumerate(targets):
                    if source_step == step and source_column == column:
                        continue
                    slot = weight_slot(source_step, step, source_column, column)
                    term = (weights_ref[slot] * plus, weights_ref[slot + 1] * minus)
                    if sums[index] is None:
                        sums[index] = term
                    else:
                        sums[index] = (sums[index][0] + term[0], sums[index][1] + term[1])
            for (plus, minus), (_, _, output, slot) in zip(sums, targets):
                outputs[output][slot, 0] = (plus + minus).astype(outputs[output].dtype)
                outputs[output][slot, 1] = (plus - minus).astype(outputs[output].dtype)

    pairs = sum(len(sources) * len(targets) for sources, targets in groups)
    moved = 2 * BLOCK * RHS * (2 * len(operands) + 2 * sum(slots))
    return pl.pallas_call(
        kernel,
        grid=(BLOCK // rows,),
        in_specs=[pl.BlockSpec(memory_space=pltpu.SMEM)]
        + [
            pl.BlockSpec((1, 2, rows, RHS), lambda i, place=place: (place, 0, i, 0))
            for _, place in operands
        ],
        out_specs=[pl.BlockSpec((count, 2, rows, RHS), lambda i: (0, 0, i, 0)) for count in slots],
        out_shape=[
            jax.ShapeDtypeStruct((count, *PIECE), dtype) for count, dtype in zip(slots, dtypes)
        ],
        cost_estimate=pl.CostEstimate(
            flops=4 * pairs * BLOCK * RHS, bytes_accessed=moved, transcendentals=0
        ),
    )(weights, *[array for array, _ in operands])


def finish(elements, base, scaled_mass, block_inverse, own, passed, near, across):
    def kernel(elements_ref, base_ref, mass_ref, inverse_ref, own_ref, passed_ref, *refs):
        near_refs, across_refs = refs[:ROLES], refs[ROLES: 2 * ROLES]
        out_ref, spectral = refs[2 * ROLES:]
        step = pl.program_id(0)
        for place in range(ROLES):
            @pl.when(step == place)
            def _():
                spectral[...] = own_ref[0] + near_refs[place][0].astype(jnp.float32)

            @pl.when(step == ROLES + place)
            def _():
                spectral[...] = passed_ref[0].astype(jnp.float32) + across_refs[place][0].astype(jnp.float32)

        for half in range(2):
            mixed = spectral[half].astype(jnp.bfloat16).astype(jnp.float32)
            residual = (base_ref[half, 0] - mass_ref[0] * mixed).astype(jnp.bfloat16)
            out_ref[half, 0] = jnp.dot(
                inverse_ref[half, 0], residual, preferred_element_type=jnp.float32
            ).astype(jnp.bfloat16)

    whole = pl.BlockSpec((1, *PIECE), lambda i, e: (0, 0, 0, 0))
    return pl.pallas_call(
        kernel,
        grid_spec=pltpu.PrefetchScalarGridSpec(
            num_scalar_prefetch=1,
            grid=(2 * ROLES,),
            in_specs=[
                pl.BlockSpec((2, 1, BLOCK, RHS), lambda i, e: (0, e[i], 0, 0)),
                pl.BlockSpec((1, BLOCK, RHS), lambda i, e: (e[i], 0, 0)),
                pl.BlockSpec((2, 1, BLOCK, BLOCK), lambda i, e: (0, e[i], 0, 0)),
                pl.BlockSpec((1, *PIECE), lambda i, e: (jnp.minimum(i, ROLES - 1), 0, 0, 0)),
                pl.BlockSpec((1, *PIECE), lambda i, e: (jnp.maximum(i - ROLES, 0), 0, 0, 0)),
            ]
            + [whole] * (2 * ROLES),
            out_specs=pl.BlockSpec((2, 1, BLOCK, RHS), lambda i, e: (0, e[i], 0, 0)),
            scratch_shapes=[pltpu.VMEM(PIECE, jnp.float32)],
        ),
        out_shape=jax.ShapeDtypeStruct((2, 2 * ROLES, BLOCK, RHS), jnp.bfloat16),
        cost_estimate=pl.CostEstimate(
            flops=4 * 2 * ROLES * BLOCK * BLOCK * RHS, bytes_accessed=10_000_000, transcendentals=0
        ),
    )(elements, base, scaled_mass, block_inverse, own, passed, *near, *across)


def from_behind(value, axis, steps):
    count = lax.axis_size(axis)
    first, last = (max(0, -steps), min(count, count - steps))
    return lax.ppermute(value, axis, [(source, source + steps) for source in range(first, last)])


def neighbour_traces(field, lower_rim, upper_rim):
    x_low = field[:, :, :, :, :, -1]
    x_high = field[:, :, :, :, :, 0]
    minus_x = jnp.concatenate([lower_rim[:, None], x_low[:, :-1]], axis=1)
    plus_x = jnp.concatenate([x_high[:, 1:], upper_rim[:, None]], axis=1)
    minus_y = jnp.roll(field[:, :, :, :, :, :, -1], 1, axis=2)
    plus_y = jnp.roll(field[:, :, :, :, :, :, 0], -1, axis=2)
    z_low = field[:, :, :, :, :, :, :, -1]
    z_high = field[:, :, :, :, :, :, :, 0]
    blank = jnp.zeros_like(z_low[:, :, :, :1])
    minus_z = jnp.concatenate([blank, z_low[:, :, :, :-1]], axis=3)
    plus_z = jnp.concatenate([z_high[:, :, :, 1:], blank], axis=3)
    return jnp.stack([minus_x, plus_x, minus_y, plus_y, minus_z, plus_z], axis=4)


def per_device(adjoint, source, block_inverse, face_partials, mass):
    member = lax.axis_index("tm")
    field = adjoint[:, 0]
    weights = lax.dynamic_index_in_dim(jnp.asarray(weight_table()), member, 0, keepdims=False)
    elements = lax.dynamic_index_in_dim(jnp.asarray(element_table()), member, 0, keepdims=False)

    def picked(first, last):
        return jnp.stack([
            lax.dynamic_index_in_dim(field, elements[place], 1, keepdims=False)
            for place in range(first, last)
        ])

    mine = picked(0, ROLES)
    other = send(picked(ROLES, 2 * ROLES), 0, 1)
    up, down = [], []
    for held in (mine, other):
        up1 = send(held[1:4], 1)
        down1 = send(held[0:3], -1)
        up2 = send(up1[1:3], 1)
        down2 = send(down1[0:2], -1)
        up3 = send(up2[1:2], 1)
        down3 = send(down2[0:1], -1)
        up.append((held, up1, up2, up3))
        down.append((held, down1, down2, down3))

    def sources(entries):
        return [
            (stream[column][level], place, step, column)
            for column in (OWN, OTHER)
            for stream, level, place, step in entries
        ]

    role_one = sources([(up, 0, 0, 0), (up, 1, 0, -1), (up, 2, 0, -2), (up, 3, 0, -3)])
    role_two = sources([(down, 0, 3, 0), (down, 1, 2, 1), (down, 2, 1, 2), (down, 3, 0, 3)])
    role_zero = sources([(up, 0, 1, 0), (up, 1, 1, -1), (up, 2, 1, -2), (down, 1, 0, 1)])
    role_three = sources([(up, 0, 2, 0), (down, 1, 1, 1), (down, 2, 0, 2), (up, 1, 2, -1)])
    bf16 = jnp.bfloat16
    f32 = jnp.float32
    here = [(0, OWN, 0), (0, OTHER, 1)]

    def ahead(sign):
        return [(2 * sign, OWN, 0), (2 * sign, OTHER, 1), (sign, OWN, 2), (sign, OTHER, 3)]

    outer_own, outer_other = combine(weights, [(role_zero, here), (role_three, here)], [f32, bf16])
    passed_outer = send(outer_other, 0, 1)
    up_sums = combine(weights, [(role_one, ahead(1))], [bf16] * 4)
    down_sums = combine(weights, [(role_two, ahead(-1))], [bf16] * 4)
    up_far, up_far_across = send(up_sums[0], 2), send(up_sums[1], 2, 1)
    down_far, down_far_across = send(down_sums[0], -2), send(down_sums[1], -2, 1)
    up_near, up_near_across = send(up_sums[2], 1), send(up_sums[3], 1, 1)
    down_near, down_near_across = send(down_sums[2], -1), send(down_sums[3], -1, 1)
    inner_own, inner_other = combine(weights, [(role_one, here), (role_two, here)], [f32, bf16])
    passed_inner = send(inner_other, 0, 1)

    elements_here = adjoint.shape[2]
    grid = field.reshape(2, LAY_DEV, EY, EZ, VARS, P1, P1, P1, RHS)
    lower_rim = from_behind(grid[:, -1, :, :, :, -1], "mesh", 1)
    upper_rim = from_behind(grid[:, 0, :, :, :, 0], "mesh", -1)
    traces = neighbour_traces(grid, lower_rim, upper_rim).reshape(2, elements_here, 6, FACE, RHS)
    coupling = jnp.einsum(
        "hefkq,hefkr->heqr", face_partials[:, 0], traces, preferred_element_type=jnp.float32
    )
    base = source[:, 0].astype(jnp.float32) - coupling
    scaled_mass = jnp.broadcast_to((OMEGA_TIME * mass)[:, :, None], (elements_here, BLOCK, RHS))

    def in_order(outer, inner):
        return jnp.concatenate([inner[0:1], outer, inner[1:2]])

    updated = finish(
        elements, base, scaled_mass, block_inverse[:, 0],
        in_order(outer_own, inner_own), in_order(passed_outer, passed_inner),
        [down_near, down_far, up_far, up_near],
        [down_near_across, down_far_across, up_far_across, up_near_across],
    )
    return updated[:, None]


def solution(mesh):
    return jax.shard_map(
        per_device,
        mesh=mesh,
        in_specs=(
            P(None, "tm", "mesh", None, None),
            P(None, "tm", "mesh", None, None),
            P(None, "tm", "mesh", None, None),
            P(None, "tm", "mesh", None, None, None),
            P("mesh", None),
        ),
        out_specs=P(None, "tm", "mesh", None, None),
        check_vma=False,
    )
```

time: 504 us -> 138 us (0.27)
  the two profiles are of different devices: /device:TPU:6 before, /device:TPU:8 now
where the time goes in v1:
time: 138 us; the launch traced here: 137 us
  starting transfers between devices  45.4 us (33%)
  waiting for transfers between devices  31.3 us (23%)
  Pallas kernels  25.1 us (18%)
  between operations  15.4 us (11%)
  local copies, waits for them, and re-layouts  12.7 us (9%)
  other arithmetic  3.64 us (3%)
  matrix products  3.34 us (2%)
    ppermute x23, starting transfers between devices, send(): return lax.ppermute(value, 'tm', column_pairs(step, swap))  42.8 us
    ppermute x23, waiting for transfers between devices, send(): return lax.ppermute(value, 'tm', column_pairs(step, swap))  31.3 us
    pallas_call x4, Pallas kernels, combine(): pl.pallas_call(kernel, grid=(BLOCK // rows,), in_specs=[pl.BlockSpec(memo...  15.8 us
    pallas_call x1, Pallas kernels, finish(): pl.pallas_call(kernel, grid_spec=pltpu.PrefetchScalarGridSpec(num_scalar_...  9.24 us
    dot_general x1, matrix products, per_device(): jnp.einsum('hefkq,hefkr->heqr', face_partials[:, 0], traces, preferred_el...  3.34 us
  transfers between devices with their start and end apart: 25, of which 7 were waited for; matrix products, arithmetic and copies ran while one was open for 9% of the time, Pallas kernels for 12%

profile of v1, /device:TPU:8, one launch (start us, length us, event | category | flops | bytes accessed | tf_op | source)
XLA Modules:
  0.0 136.9 jit_solution(3586671963932574227)
XLA Ops:
  0.0 1.2 constant_dynamic-slice_fusion.1
  1.2 0.7 fusion.10
  16.7 1.5 %dynamic-slice_bitcast_fusion.3 = (bf16[1,2,320,128]{3,2,1,0:T(8,128)(2,1)S(1)}, bf16[1,2,320,128]{3,2,1,0:T(8,128)(2,1)S(1)}, bf16[1,2,320,128]{3,2,1,0:T(8,128...) fusion(bf16[2,1,8,320,128]{4,3,2,1,0:T(8,128)(2,1)} %param.7, ...), kind=kLoop, calls=%fused_computation.20 | loop fusion | bytes 2621472 | tf_op jit(solution)/shard_map/stack | solution.py:213
  18.4 2.3 %collective-permute-start.5 = (bf16[4,2,320,128]{3,2,1,0:T(8,128)(2,1)S(1)}, bf16[4,2,320,128]{3,2,1,0:T(8,128)(2,1)S(1)}, u32[]{:S(2)}, u32[]{:S(2)}) collective-permute-start(bf16[4,2,320,128]{3,2,1,0:T(8,128)(2,1)S(1)} %pad_maximum_fusion.2), channel_id=1, source_target_pairs={{0,16},{16,0},{32,48},{48,32},{64,80},{80,64},{96,112},{112,96},{1... | collective-permute-start | bytes 1966088 | tf_op jit(solution)/shard_map/ppermute | solution.py:79
  20.7 0.3 collective-permute-start.2
  21.0 4.0 %collective-permute-start.9 = (bf16[3,2,320,128]{3,2,1,0:T(8,128)(2,1)S(1)}, bf16[3,2,320,128]{3,2,1,0:T(8,128)(2,1)S(1)}, u32[]{:S(2)}, u32[]{:S(2)}) collective-permute-start(bf16[3,2,320,128]{3,2,1,0:T(8,128)(2,1)S(1)} %get-tuple-element.49), channel_id=1, source_target_pairs={{0,224},{16,240},{32,0},{48,16},{64,32},{80,48},{96,64},{112,80},{... | collective-permute-start | bytes 1474568 | tf_op jit(solution)/shard_map/ppermute | solution.py:79
  25.0 0.2 slice_bitcast_fusion.2
  25.2 1.3 collective-permute-start
  26.6 1.3 collective-permute-start.1
  27.9 1.3 fusion.6
  29.2 0.2 slice_bitcast_fusion
  30.4 8.1 %collective-permute-done.5.refs_4_.refs_12_ = bf16[4,2,320,128]{3,2,1,0:T(8,128)(2,1)S(1)} collective-permute-done((bf16[4,2,320,128]{3,2,1,0:T(8,128)(2,1)S(1)}, bf16[4,2,320,128]{3,2,1,0:T(8,128)(2,1)S(1)}, u32[]{:S(2)}, u32[]{:S(2)}) %collective-permute-start.5) | collective-permute-done | bytes 655392 | tf_op jit(solution)/shard_map/ppermute | solution.py:79
  38.5 2.0 %collective-permute-start.6 = (bf16[3,2,320,128]{3,2,1,0:T(8,128)(2,1)S(1)}, bf16[3,2,320,128]{3,2,1,0:T(8,128)(2,1)S(1)}, u32[]{:S(2)}, u32[]{:S(2)}) collective-permute-start(bf16[3,2,320,128]{3,2,1,0:T(8,128)(2,1)S(1)} %get-tuple-element.46), channel_id=1, source_target_pairs={{0,32},{16,48},{32,64},{48,80},{64,96},{80,112},{96,128},{112,144}... | collective-permute-start | bytes 1474568 | tf_op jit(solution)/shard_map/ppermute | solution.py:79
  40.5 4.0 %collective-permute-start.12 = (bf16[3,2,320,128]{3,2,1,0:T(8,128)(2,1)S(1)}, bf16[3,2,320,128]{3,2,1,0:T(8,128)(2,1)S(1)}, u32[]{:S(2)}, u32[]{:S(2)}) collective-permute-start(bf16[3,2,320,128]{3,2,1,0:T(8,128)(2,1)S(1)} %get-tuple-element.45), channel_id=1, source_target_pairs={{0,224},{16,240},{32,0},{48,16},{64,32},{80,48},{96,64},{112,80},{... | collective-permute-start | bytes 1474568 | tf_op jit(solution)/shard_map/ppermute | solution.py:79
  45.2 1.3 fusion.4.weights_ref
  46.5 0.9 pad_maximum_fusion.1.refs_0_.refs_8_
  47.7 3.3 %collective-permute-start.10 = (bf16[2,2,320,128]{3,2,1,0:T(8,128)(2,1)S(1)}, bf16[2,2,320,128]{3,2,1,0:T(8,128)(2,1)S(1)}, u32[]{:S(2)}, u32[]{:S(2)}) collective-permute-start(bf16[2,2,320,128]{3,2,1,0:T(8,128)(2,1)S(1)} %slice.169), channel_id=1, source_target_pairs={{0,224},{16,240},{32,0},{48,16},{64,32},{80,48},{96,64},{112,80},{... | collective-permute-start | bytes 983048 | tf_op jit(solution)/shard_map/ppermute | solution.py:79
  51.0 5.6 %collective-permute-done.6.refs_5_.refs_15_ = bf16[3,2,320,128]{3,2,1,0:T(8,128)(2,1)S(1)} collective-permute-done((bf16[3,2,320,128]{3,2,1,0:T(8,128)(2,1)S(1)}, bf16[3,2,320,128]{3,2,1,0:T(8,128)(2,1)S(1)}, u32[]{:S(2)}, u32[]{:S(2)}) %collective-permute-start.6) | collective-permute-done | bytes 491552 | tf_op jit(solution)/shard_map/ppermute | solution.py:79
  56.8 3.3 %collective-permute-start.13 = (bf16[2,2,320,128]{3,2,1,0:T(8,128)(2,1)S(1)}, bf16[2,2,320,128]{3,2,1,0:T(8,128)(2,1)S(1)}, u32[]{:S(2)}, u32[]{:S(2)}) collective-permute-start(bf16[2,2,320,128]{3,2,1,0:T(8,128)(2,1)S(1)} %slice.172), channel_id=1, source_target_pairs={{0,224},{16,240},{32,0},{48,16},{64,32},{80,48},{96,64},{112,80},{... | collective-permute-start | bytes 983048 | tf_op jit(solution)/shard_map/ppermute | solution.py:79
  60.2 3.4 %collective-permute-done.3.refs_2_ = bf16[2,2,320,128]{3,2,1,0:T(8,128)(2,1)S(1)} collective-permute-done((bf16[2,2,320,128]{3,2,1,0:T(8,128)(2,1)S(1)}, bf16[2,2,320,128]{3,2,1,0:T(8,128)(2,1)S(1)}, u32[]{:S(2)}, u32[]{:S(2)}) %collective-permute-start.3) | collective-permute-done | bytes 327712 | tf_op jit(solution)/shard_map/ppermute | solution.py:79
  63.8 3.5 %collective-permute-start.11 = (bf16[1,2,320,128]{3,2,1,0:T(8,128)(2,1)S(1)}, bf16[1,2,320,128]{3,2,1,0:T(8,128)(2,1)S(1)}, u32[]{:S(2)}, u32[]{:S(2)}) collective-permute-start(bf16[1,2,320,128]{3,2,1,0:T(8,128)(2,1)S(1)} %slice.170), channel_id=1, source_target_pairs={{0,224},{16,240},{32,0},{48,16},{64,32},{80,48},{96,64},{112,80},{... | collective-permute-start | bytes 491528 | tf_op jit(solution)/shard_map/ppermute | solution.py:79
  67.2 3.4 %collective-permute-done.7.refs_6_ = bf16[2,2,320,128]{3,2,1,0:T(8,128)(2,1)S(1)} collective-permute-done((bf16[2,2,320,128]{3,2,1,0:T(8,128)(2,1)S(1)}, bf16[2,2,320,128]{3,2,1,0:T(8,128)(2,1)S(1)}, u32[]{:S(2)}, u32[]{:S(2)}) %collective-permute-start.7) | collective-permute-done | bytes 327712 | tf_op jit(solution)/shard_map/ppermute | solution.py:79
  70.8 3.3 %collective-permute-start.14 = (bf16[1,2,320,128]{3,2,1,0:T(8,128)(2,1)S(1)}, bf16[1,2,320,128]{3,2,1,0:T(8,128)(2,1)S(1)}, u32[]{:S(2)}, u32[]{:S(2)}) collective-permute-start(bf16[1,2,320,128]{3,2,1,0:T(8,128)(2,1)S(1)} %slice.173), channel_id=1, source_target_pairs={{0,224},{16,240},{32,0},{48,16},{64,32},{80,48},{96,64},{112,80},{... | collective-permute-start | bytes 491528 | tf_op jit(solution)/shard_map/ppermute | solution.py:79
  74.1 3.3 %bitcast_subtract_fusion.base_ref = f32[2,8,320,128]{3,2,1,0:T(8,128)} fusion(bf16[2,8,6,80,128]{4,3,2,1,0:T(8,128)(2,1)S(1)} %constant_dynamic-update-slice_fusion, bf16[2,1,8,6,80,320]{5,4,3,2,1,0:T(8,128)(2,1)S(1)} %bitcast.77, bf16[2,1,8,320,128]{4,3,2,1,0:T(8,128)(2,1)S(1)} %copy-done.10), kind=kOutput, calls=%fused_computation.2 | convolution fusion | flops 630456320 | bytes 10813440 | tf_op jit(solution)/shard_map/hefkq,hefkr->heqr/dot_general | solution.py:265
  77.4 4.1 %shard_map.74 = (f32[2,2,320,128]{3,2,1,0:T(8,128)}, bf16[2,2,320,128]{3,2,1,0:T(8,128)(2,1)}) custom-call(f32[280]{0:T(512)} %fusion.4.weights_ref, bf16[4,2,320,128]{3,2,1,0:T(8,128)(2,1)} %pad_maximum_fusion.1.refs_0_.refs_8_, bf16[3,2,320,128]{3,2,1,0:T(8,128)(2,1)} %copy-done.3, bf16[2,2,320,128]{3,2,1,0:T(8,128)(2,1)} %copy-done.7, ...), custom_call_target="tpu_custom_call" | custom-call | flops 5242880 | bytes 3276800 | tf_op jit(solution)/shard_map/pallas_call | solution.py:122
  81.6 0.5 collective-permute-start.16
  82.1 0.7 copy-done.12
  82.8 0.7 copy-done.14
  83.4 3.7 %shard_map.76 = (bf16[1,2,320,128]{3,2,1,0:T(8,128)(2,1)}, bf16[1,2,320,128]{3,2,1,0:T(8,128)(2,1)}, bf16[1,2,320,128]{3,2,1,0:T(8,128)(2,1)}, bf16[1,2,320,128]{3,2,1,0:T(8,128)(2,1)}) custom-call(f32[280]{0:T(512)} %fusion.4.weights_ref, bf16[4,2,320,128]{3,2,1,0:T(8,128)(2,1)} %pad_maximum_fusion.1.refs_0_.refs_8_, bf16[3,2,320,128]{3,2,1,0:T(8,128)(2,1)} %copy-done.3, ...), custom_call_target="tpu_custom_call" | custom-call | flops 5242880 | bytes 1966080 | tf_op jit(solution)/shard_map/pallas_call | solution.py:122
  87.3 2.2 %collective-permute-start.20 = (bf16[1,2,320,128]{3,2,1,0:T(8,128)(2,1)}, bf16[1,2,320,128]{3,2,1,0:T(8,128)(2,1)S(1)}, u32[]{:S(2)}, u32[]{:S(2)}) collective-permute-start(bf16[1,2,320,128]{3,2,1,0:T(8,128)(2,1)} %get-tuple-element.24), channel_id=1, source_target_pairs={{0,32},{16,48},{32,64},{48,80},{64,96},{80,112},{96,128},{112,144}... | collective-permute-start | bytes 491528 | tf_op jit(solution)/shard_map/ppermute | solution.py:79
  89.5 3.7 %collective-permute-start.23 = (bf16[1,2,320,128]{3,2,1,0:T(8,128)(2,1)}, bf16[1,2,320,128]{3,2,1,0:T(8,128)(2,1)S(1)}, u32[]{:S(2)}, u32[]{:S(2)}) collective-permute-start(bf16[1,2,320,128]{3,2,1,0:T(8,128)(2,1)} %get-tuple-element.27), channel_id=1, source_target_pairs={{0,80},{16,64},{32,112},{48,96},{64,144},{80,128},{96,176},{112,16... | collective-permute-start | bytes 491528 | tf_op jit(solution)/shard_map/ppermute | solution.py:79
  93.2 0.7 copy-done.13
  93.9 4.2 %shard_map.73 = (f32[2,2,320,128]{3,2,1,0:T(8,128)}, bf16[2,2,320,128]{3,2,1,0:T(8,128)(2,1)}) custom-call(f32[280]{0:T(512)} %fusion.4.weights_ref, bf16[4,2,320,128]{3,2,1,0:T(8,128)(2,1)} %pad_maximum_fusion.1.refs_0_.refs_8_, bf16[3,2,320,128]{3,2,1,0:T(8,128)(2,1)} %copy-done.3, bf16[2,2,320,128]{3,2,1,0:T(8,128)(2,1)} %copy-done.7, ...), custom_call_target="tpu_custom_call" | custom-call | flops 5242880 | bytes 3276800 | tf_op jit(solution)/shard_map/pallas_call | solution.py:122
  98.0 0.5 collective-permute-start.15
  98.6 1.1 fusion.7
  99.7 3.8 %shard_map.75 = (bf16[1,2,320,128]{3,2,1,0:T(8,128)(2,1)}, bf16[1,2,320,128]{3,2,1,0:T(8,128)(2,1)}, bf16[1,2,320,128]{3,2,1,0:T(8,128)(2,1)}, bf16[1,2,320,128]{3,2,1,0:T(8,128)(2,1)}) custom-call(f32[280]{0:T(512)} %fusion.4.weights_ref, bf16[4,2,320,128]{3,2,1,0:T(8,128)(2,1)} %pad_maximum_fusion.1.refs_0_.refs_8_, bf16[3,2,320,128]{3,2,1,0:T(8,128)(2,1)} %copy-done.2, ...), custom_call_target="tpu_custom_call" | custom-call | flops 5242880 | bytes 1966080 | tf_op jit(solution)/shard_map/pallas_call | solution.py:122
  103.6 1.2 pad_maximum_fusion.own_ref
  104.8 1.6 %collective-permute-start.24 = (bf16[1,2,320,128]{3,2,1,0:T(8,128)(2,1)S(1)}, bf16[1,2,320,128]{3,2,1,0:T(8,128)(2,1)S(1)}, u32[]{:S(2)}, u32[]{:S(2)}) collective-permute-start(bf16[1,2,320,128]{3,2,1,0:T(8,128)(2,1)S(1)} %copy-done.25), channel_id=1, source_target_pairs={{0,48},{16,32},{32,80},{48,64},{64,112},{80,96},{96,144},{112,128}... | collective-permute-start | bytes 491528 | tf_op jit(solution)/shard_map/ppermute | solution.py:79
  106.4 2.7 %collective-permute-start.17 = (bf16[1,2,320,128]{3,2,1,0:T(8,128)(2,1)S(1)}, bf16[1,2,320,128]{3,2,1,0:T(8,128)(2,1)S(1)}, u32[]{:S(2)}, u32[]{:S(2)}) collective-permute-start(bf16[1,2,320,128]{3,2,1,0:T(8,128)(2,1)S(1)} %copy-done.29), channel_id=1, source_target_pairs={{0,224},{16,240},{32,0},{48,16},{64,32},{80,48},{96,64},{112,80},{... | collective-permute-start | bytes 491528 | tf_op jit(solution)/shard_map/ppermute | solution.py:79
  109.1 1.5 %collective-permute-start.18 = (bf16[1,2,320,128]{3,2,1,0:T(8,128)(2,1)S(1)}, bf16[1,2,320,128]{3,2,1,0:T(8,128)(2,1)S(1)}, u32[]{:S(2)}, u32[]{:S(2)}) collective-permute-start(bf16[1,2,320,128]{3,2,1,0:T(8,128)(2,1)S(1)} %copy-done.28), channel_id=1, source_target_pairs={{0,192},{16,208},{32,224},{48,240},{64,0},{80,16},{96,32},{112,48}... | collective-permute-start | bytes 491528 | tf_op jit(solution)/shard_map/ppermute | solution.py:79
  110.6 0.5 collective-permute-start.21
  111.1 3.2 %collective-permute-start.22 = (bf16[1,2,320,128]{3,2,1,0:T(8,128)(2,1)S(1)}, bf16[1,2,320,128]{3,2,1,0:T(8,128)(2,1)S(1)}, u32[]{:S(2)}, u32[]{:S(2)}) collective-permute-start(bf16[1,2,320,128]{3,2,1,0:T(8,128)(2,1)S(1)} %copy-done.26), channel_id=1, source_target_pairs={{0,208},{16,192},{32,240},{48,224},{64,16},{80,0},{96,48},{112,32}... | collective-permute-start | bytes 491528 | tf_op jit(solution)/shard_map/ppermute | solution.py:79
  114.3 0.9 pad_maximum_fusion.3.passed_ref
  115.3 5.0 %collective-permute-done.18.refs_1_ = bf16[1,2,320,128]{3,2,1,0:T(8,128)(2,1)S(1)} collective-permute-done((bf16[1,2,320,128]{3,2,1,0:T(8,128)(2,1)S(1)}, bf16[1,2,320,128]{3,2,1,0:T(8,128)(2,1)S(1)}, u32[]{:S(2)}, u32[]{:S(2)}) %collective-permute-start.18) | collective-permute-done | bytes 163872 | tf_op jit(solution)/shard_map/ppermute | solution.py:79
  120.2 2.4 %collective-permute-done.21.refs_4_ = bf16[1,2,320,128]{3,2,1,0:T(8,128)(2,1)S(1)} collective-permute-done((bf16[1,2,320,128]{3,2,1,0:T(8,128)(2,1)S(1)}, bf16[1,2,320,128]{3,2,1,0:T(8,128)(2,1)S(1)}, u32[]{:S(2)}, u32[]{:S(2)}) %collective-permute-start.21) | collective-permute-done | bytes 163872 | tf_op jit(solution)/shard_map/ppermute | solution.py:79
  122.6 3.5 %collective-permute-done.22.refs_5_ = bf16[1,2,320,128]{3,2,1,0:T(8,128)(2,1)S(1)} collective-permute-done((bf16[1,2,320,128]{3,2,1,0:T(8,128)(2,1)S(1)}, bf16[1,2,320,128]{3,2,1,0:T(8,128)(2,1)S(1)}, u32[]{:S(2)}, u32[]{:S(2)}) %collective-permute-start.22) | collective-permute-done | bytes 163872 | tf_op jit(solution)/shard_map/ppermute | solution.py:79
  126.1 1.5 %broadcast_in_dim.4.mass_ref = f32[8,320,128]{2,1,0:T(8,128)} broadcast(f32[8,320]{1,0:T(8,128)S(1)} %broadcast_multiply_fusion), dimensions={0,1} | broadcast | bytes 1320960 | tf_op jit(solution)/shard_map/broadcast_in_dim | solution.py:269
  127.6 9.2 %shard_map.77 = bf16[2,8,320,128]{3,2,1,0:T(8,128)(2,1)} custom-call(s32[8]{0:T(128)} %get-tuple-element.52.elements_ref, f32[2,8,320,128]{3,2,1,0:T(8,128)} %bitcast_subtract_fusion.base_ref, f32[8,320,128]{2,1,0:T(8,128)} %broadcast_in_dim.4.mass_ref, bf16[2,8,320,320]{3,2,1,0:T(8,128)(2,1)} %bitcast.78, f32[4,2,320,128]{3,2,1,0:T(8,128)} %pad_maximum_fusion.own_ref, ...), custom_call_target="tpu_custom_call" | custom-call | flops 419430400 | bytes 10000000 | tf_op jit(solution)/shard_map/pallas_call | solution.py:162
  (115 shorter events, 2.7 us)
Async XLA Ops:
  18.2 6.8 %copy-start.1 = (bf16[2,1,8,320,128]{4,3,2,1,0:T(8,128)(2,1)S(1)}, bf16[2,1,8,320,128]{4,3,2,1,0:T(8,128)(2,1)}, u32[]{:S(2)}) copy-start(bf16[2,1,8,320,128]{4,3,2,1,0:T(8,128)(2,1)} %param.7) | copy-start | bytes 3932164
  18.4 20.1 %collective-permute-start.5 = (bf16[4,2,320,128]{3,2,1,0:T(8,128)(2,1)S(1)}, bf16[4,2,320,128]{3,2,1,0:T(8,128)(2,1)S(1)}, u32[]{:S(2)}, u32[]{:S(2)}) collective-permute-start(bf16[4,2,320,128]{3,2,1,0:T(8,128)(2,1)S(1)} %pad_maximum_fusion.2), channel_id=1, source_target_pairs={{0,16},{16,0},{32,48},{48,32},{64,80},{80,64},{96,112},{112,96},{1... | collective-permute-start | bytes 1966088 | tf_op jit(solution)/shard_map/ppermute | solution.py:79
  20.7 26.8 %collective-permute-start.2 = (bf16[3,2,320,128]{3,2,1,0:T(8,128)(2,1)S(1)}, bf16[3,2,320,128]{3,2,1,0:T(8,128)(2,1)S(1)}, u32[]{:S(2)}, u32[]{:S(2)}) collective-permute-start(bf16[3,2,320,128]{3,2,1,0:T(8,128)(2,1)S(1)} %get-tuple-element.50), channel_id=1, source_target_pairs={{0,32},{16,48},{32,64},{48,80},{64,96},{80,112},{96,128},{112,144}... | collective-permute-start | bytes 1474568 | tf_op jit(solution)/shard_map/ppermute | solution.py:79
  21.0 26.7 %collective-permute-start.9 = (bf16[3,2,320,128]{3,2,1,0:T(8,128)(2,1)S(1)}, bf16[3,2,320,128]{3,2,1,0:T(8,128)(2,1)S(1)}, u32[]{:S(2)}, u32[]{:S(2)}) collective-permute-start(bf16[3,2,320,128]{3,2,1,0:T(8,128)(2,1)S(1)} %get-tuple-element.49), channel_id=1, source_target_pairs={{0,224},{16,240},{32,0},{48,16},{64,32},{80,48},{96,64},{112,80},{... | collective-permute-start | bytes 1474568 | tf_op jit(solution)/shard_map/ppermute | solution.py:79
  25.2 15.3 %collective-permute-start = (bf16[2,4,2,5,4,4,128]{6,5,4,3,2,1,0:T(4,128)(2,1)S(1)}, bf16[2,4,2,5,4,4,128]{6,5,4,3,2,1,0:T(4,128)(2,1)S(1)}, u32[]{:S(2)}, u32[]{:S(2)}) collective-permute-start(bf16[2,4,2,5,4,4,128]{6,5,4,3,2,1,0:T(4,128)(2,1)S(1)} %get-tuple-element.42), channel_id=1, source_target_pairs={{0,1},{1,2},{2,3},{3,4},{4,5},{5,6},{6,7},{7,8},{8,9},{9,10},{10,1... | collective-permute-start | bytes 983048 | tf_op jit(solution)/shard_map/ppermute | solution.py:188
  26.6 20.9 %collective-permute-start.1 = (bf16[2,4,2,5,4,4,128]{6,5,4,3,2,1,0:T(4,128)(2,1)S(1)}, bf16[2,4,2,5,4,4,128]{6,5,4,3,2,1,0:T(4,128)(2,1)S(1)}, u32[]{:S(2)}, u32[]{:S(2)}) collective-permute-start(bf16[2,4,2,5,4,4,128]{6,5,4,3,2,1,0:T(4,128)(2,1)S(1)} %get-tuple-element.41), channel_id=1, source_target_pairs={{1,0},{2,1},{3,2},{4,3},{5,4},{6,5},{7,6},{8,7},{9,8},{10,9},{11,1... | collective-permute-start | bytes 983048 | tf_op jit(solution)/shard_map/ppermute | solution.py:188
  29.9 44.2 %slice-start = ((s8[5898240]{0:T(1024)(128)(4,1)}), s8[4194304]{0:T(1024)(128)(4,1)S(1)}, s32[]{:S(2)}) async-start(s8[5898240]{0:T(1024)(128)(4,1)} %bitcast.76), calls=%async_computation | async-start | bytes 8388608
  38.4 6.7 %copy-start = (bf16[4,2,320,128]{3,2,1,0:T(8,128)(2,1)}, bf16[4,2,320,128]{3,2,1,0:T(8,128)(2,1)S(1)}, u32[]{:S(2)}) copy-start(bf16[4,2,320,128]{3,2,1,0:T(8,128)(2,1)S(1)} %collective-permute-done.5.refs_4_.refs_12_) | copy-start | bytes 1966084
  38.5 18.1 %collective-permute-start.6 = (bf16[3,2,320,128]{3,2,1,0:T(8,128)(2,1)S(1)}, bf16[3,2,320,128]{3,2,1,0:T(8,128)(2,1)S(1)}, u32[]{:S(2)}, u32[]{:S(2)}) collective-permute-start(bf16[3,2,320,128]{3,2,1,0:T(8,128)(2,1)S(1)} %get-tuple-element.46), channel_id=1, source_target_pairs={{0,32},{16,48},{32,64},{48,80},{64,96},{80,112},{96,128},{112,144}... | collective-permute-start | bytes 1474568 | tf_op jit(solution)/shard_map/ppermute | solution.py:79
  40.5 16.2 %collective-permute-start.12 = (bf16[3,2,320,128]{3,2,1,0:T(8,128)(2,1)S(1)}, bf16[3,2,320,128]{3,2,1,0:T(8,128)(2,1)S(1)}, u32[]{:S(2)}, u32[]{:S(2)}) collective-permute-start(bf16[3,2,320,128]{3,2,1,0:T(8,128)(2,1)S(1)} %get-tuple-element.45), channel_id=1, source_target_pairs={{0,224},{16,240},{32,0},{48,16},{64,32},{80,48},{96,64},{112,80},{... | collective-permute-start | bytes 1474568 | tf_op jit(solution)/shard_map/ppermute | solution.py:79
  46.5 27.6 %slice-start.1 = ((s8[5898240]{0:T(1024)(128)(4,1)}), s8[1703936]{0:T(1024)(128)(4,1)S(1)}, s32[]{:S(2)}) async-start(s8[5898240]{0:T(1024)(128)(4,1)} %bitcast.76), calls=%async_computation.1 | async-start | bytes 3407872
  47.5 12.6 %copy-start.3 = (bf16[3,2,320,128]{3,2,1,0:T(8,128)(2,1)}, bf16[3,2,320,128]{3,2,1,0:T(8,128)(2,1)S(1)}, u32[]{:S(2)}) copy-start(bf16[3,2,320,128]{3,2,1,0:T(8,128)(2,1)S(1)} %collective-permute-done.2.refs_1_.refs_11_) | copy-start | bytes 1474564
  47.6 16.0 %collective-permute-start.3 = (bf16[2,2,320,128]{3,2,1,0:T(8,128)(2,1)S(1)}, bf16[2,2,320,128]{3,2,1,0:T(8,128)(2,1)S(1)}, u32[]{:S(2)}, u32[]{:S(2)}) collective-permute-start(bf16[2,2,320,128]{3,2,1,0:T(8,128)(2,1)S(1)} %slice.164), channel_id=1, source_target_pairs={{0,32},{16,48},{32,64},{48,80},{64,96},{80,112},{96,128},{112,144}... | collective-permute-start | bytes 983048 | tf_op jit(solution)/shard_map/ppermute | solution.py:79
  47.7 12.5 %copy-start.2 = (bf16[3,2,320,128]{3,2,1,0:T(8,128)(2,1)}, bf16[3,2,320,128]{3,2,1,0:T(8,128)(2,1)S(1)}, u32[]{:S(2)}) copy-start(bf16[3,2,320,128]{3,2,1,0:T(8,128)(2,1)S(1)} %collective-permute-done.9.refs_9_.refs_3_.refs_1_) | copy-start | bytes 1474564
  47.7 16.0 %collective-permute-start.10 = (bf16[2,2,320,128]{3,2,1,0:T(8,128)(2,1)S(1)}, bf16[2,2,320,128]{3,2,1,0:T(8,128)(2,1)S(1)}, u32[]{:S(2)}, u32[]{:S(2)}) collective-permute-start(bf16[2,2,320,128]{3,2,1,0:T(8,128)(2,1)S(1)} %slice.169), channel_id=1, source_target_pairs={{0,224},{16,240},{32,0},{48,16},{64,32},{80,48},{96,64},{112,80},{... | collective-permute-start | bytes 983048 | tf_op jit(solution)/shard_map/ppermute | solution.py:79
  56.6 7.2 %copy-start.5 = (bf16[3,2,320,128]{3,2,1,0:T(8,128)(2,1)}, bf16[3,2,320,128]{3,2,1,0:T(8,128)(2,1)S(1)}, u32[]{:S(2)}) copy-start(bf16[3,2,320,128]{3,2,1,0:T(8,128)(2,1)S(1)} %collective-permute-done.6.refs_5_.refs_15_) | copy-start | bytes 1474564
  56.6 17.4 %copy-start.10 = (bf16[2,1,8,320,128]{4,3,2,1,0:T(8,128)(2,1)S(1)}, bf16[2,1,8,320,128]{4,3,2,1,0:T(8,128)(2,1)}, u32[]{:S(2)}) copy-start(bf16[2,1,8,320,128]{4,3,2,1,0:T(8,128)(2,1)} %param.8) | copy-start | bytes 3932164
  56.6 14.0 %collective-permute-start.7 = (bf16[2,2,320,128]{3,2,1,0:T(8,128)(2,1)S(1)}, bf16[2,2,320,128]{3,2,1,0:T(8,128)(2,1)S(1)}, u32[]{:S(2)}, u32[]{:S(2)}) collective-permute-start(bf16[2,2,320,128]{3,2,1,0:T(8,128)(2,1)S(1)} %slice.167), channel_id=1, source_target_pairs={{0,32},{16,48},{32,64},{48,80},{64,96},{80,112},{96,128},{112,144}... | collective-permute-start | bytes 983048 | tf_op jit(solution)/shard_map/ppermute | solution.py:79
  56.7 14.0 %copy-start.4 = (bf16[3,2,320,128]{3,2,1,0:T(8,128)(2,1)}, bf16[3,2,320,128]{3,2,1,0:T(8,128)(2,1)S(1)}, u32[]{:S(2)}) copy-start(bf16[3,2,320,128]{3,2,1,0:T(8,128)(2,1)S(1)} %collective-permute-done.12.refs_13_.refs_7_.refs_5_) | copy-start | bytes 1474564
  56.8 13.9 %collective-permute-start.13 = (bf16[2,2,320,128]{3,2,1,0:T(8,128)(2,1)S(1)}, bf16[2,2,320,128]{3,2,1,0:T(8,128)(2,1)S(1)}, u32[]{:S(2)}, u32[]{:S(2)}) collective-permute-start(bf16[2,2,320,128]{3,2,1,0:T(8,128)(2,1)S(1)} %slice.172), channel_id=1, source_target_pairs={{0,224},{16,240},{32,0},{48,16},{64,32},{80,48},{96,64},{112,80},{... | collective-permute-start | bytes 983048 | tf_op jit(solution)/shard_map/ppermute | solution.py:79
  63.6 13.8 %copy-start.7 = (bf16[2,2,320,128]{3,2,1,0:T(8,128)(2,1)}, bf16[2,2,320,128]{3,2,1,0:T(8,128)(2,1)S(1)}, u32[]{:S(2)}) copy-start(bf16[2,2,320,128]{3,2,1,0:T(8,128)(2,1)S(1)} %collective-permute-done.3.refs_2_) | copy-start | bytes 983044
  63.6 18.5 %collective-permute-start.4 = (bf16[1,2,320,128]{3,2,1,0:T(8,128)(2,1)S(1)}, bf16[1,2,320,128]{3,2,1,0:T(8,128)(2,1)S(1)}, u32[]{:S(2)}, u32[]{:S(2)}) collective-permute-start(bf16[1,2,320,128]{3,2,1,0:T(8,128)(2,1)S(1)} %slice.165), channel_id=1, source_target_pairs={{0,32},{16,48},{32,64},{48,80},{64,96},{80,112},{96,128},{112,144}... | collective-permute-start | bytes 491528 | tf_op jit(solution)/shard_map/ppermute | solution.py:79
  63.7 13.7 %copy-start.6 = (bf16[2,2,320,128]{3,2,1,0:T(8,128)(2,1)}, bf16[2,2,320,128]{3,2,1,0:T(8,128)(2,1)S(1)}, u32[]{:S(2)}) copy-start(bf16[2,2,320,128]{3,2,1,0:T(8,128)(2,1)S(1)} %collective-permute-done.10.refs_10_.refs_2_) | copy-start | bytes 983044
  63.8 25.7 %collective-permute-start.11 = (bf16[1,2,320,128]{3,2,1,0:T(8,128)(2,1)S(1)}, bf16[1,2,320,128]{3,2,1,0:T(8,128)(2,1)S(1)}, u32[]{:S(2)}, u32[]{:S(2)}) collective-permute-start(bf16[1,2,320,128]{3,2,1,0:T(8,128)(2,1)S(1)} %slice.170), channel_id=1, source_target_pairs={{0,224},{16,240},{32,0},{48,16},{64,32},{80,48},{96,64},{112,80},{... | collective-permute-start | bytes 491528 | tf_op jit(solution)/shard_map/ppermute | solution.py:79
  70.6 6.8 %copy-start.9 = (bf16[2,2,320,128]{3,2,1,0:T(8,128)(2,1)}, bf16[2,2,320,128]{3,2,1,0:T(8,128)(2,1)S(1)}, u32[]{:S(2)}) copy-start(bf16[2,2,320,128]{3,2,1,0:T(8,128)(2,1)S(1)} %collective-permute-done.7.refs_6_) | copy-start | bytes 983044
  70.6 11.5 %collective-permute-start.8 = (bf16[1,2,320,128]{3,2,1,0:T(8,128)(2,1)S(1)}, bf16[1,2,320,128]{3,2,1,0:T(8,128)(2,1)S(1)}, u32[]{:S(2)}, u32[]{:S(2)}) collective-permute-start(bf16[1,2,320,128]{3,2,1,0:T(8,128)(2,1)S(1)} %slice.168), channel_id=1, source_target_pairs={{0,32},{16,48},{32,64},{48,80},{64,96},{80,112},{96,128},{112,144}... | collective-permute-start | bytes 491528 | tf_op jit(solution)/shard_map/ppermute | solution.py:79
  70.7 6.7 %copy-start.8 = (bf16[2,2,320,128]{3,2,1,0:T(8,128)(2,1)}, bf16[2,2,320,128]{3,2,1,0:T(8,128)(2,1)S(1)}, u32[]{:S(2)}) copy-start(bf16[2,2,320,128]{3,2,1,0:T(8,128)(2,1)S(1)} %collective-permute-done.13.refs_14_.refs_6_) | copy-start | bytes 983044
  70.8 22.4 %collective-permute-start.14 = (bf16[1,2,320,128]{3,2,1,0:T(8,128)(2,1)S(1)}, bf16[1,2,320,128]{3,2,1,0:T(8,128)(2,1)S(1)}, u32[]{:S(2)}, u32[]{:S(2)}) collective-permute-start(bf16[1,2,320,128]{3,2,1,0:T(8,128)(2,1)S(1)} %slice.173), channel_id=1, source_target_pairs={{0,224},{16,240},{32,0},{48,16},{64,32},{80,48},{96,64},{112,80},{... | collective-permute-start | bytes 491528 | tf_op jit(solution)/shard_map/ppermute | solution.py:79
  81.6 23.2 %collective-permute-start.16 = (bf16[2,2,320,128]{3,2,1,0:T(8,128)(2,1)}, bf16[2,2,320,128]{3,2,1,0:T(8,128)(2,1)S(1)}, u32[]{:S(2)}, u32[]{:S(2)}) collective-permute-start(bf16[2,2,320,128]{3,2,1,0:T(8,128)(2,1)} %get-tuple-element.20), channel_id=1, source_target_pairs={{0,16},{16,0},{32,48},{48,32},{64,80},{80,64},{96,112},{112,96},{1... | collective-permute-start | bytes 983048 | tf_op jit(solution)/shard_map/ppermute | solution.py:79
  87.2 19.2 %collective-permute-start.19 = (bf16[1,2,320,128]{3,2,1,0:T(8,128)(2,1)}, bf16[1,2,320,128]{3,2,1,0:T(8,128)(2,1)S(1)}, u32[]{:S(2)}, u32[]{:S(2)}) collective-permute-start(bf16[1,2,320,128]{3,2,1,0:T(8,128)(2,1)} %get-tuple-element.23), channel_id=1, source_target_pairs={{0,64},{16,80},{32,96},{48,112},{64,128},{80,144},{96,160},{112,17... | collective-permute-start | bytes 491528 | tf_op jit(solution)/shard_map/ppermute | solution.py:79
  87.3 21.8 %collective-permute-start.20 = (bf16[1,2,320,128]{3,2,1,0:T(8,128)(2,1)}, bf16[1,2,320,128]{3,2,1,0:T(8,128)(2,1)S(1)}, u32[]{:S(2)}, u32[]{:S(2)}) collective-permute-start(bf16[1,2,320,128]{3,2,1,0:T(8,128)(2,1)} %get-tuple-element.24), channel_id=1, source_target_pairs={{0,32},{16,48},{32,64},{48,80},{64,96},{80,112},{96,128},{112,144}... | collective-permute-start | bytes 491528 | tf_op jit(solution)/shard_map/ppermute | solution.py:79
  89.5 21.1 %collective-permute-start.23 = (bf16[1,2,320,128]{3,2,1,0:T(8,128)(2,1)}, bf16[1,2,320,128]{3,2,1,0:T(8,128)(2,1)S(1)}, u32[]{:S(2)}, u32[]{:S(2)}) collective-permute-start(bf16[1,2,320,128]{3,2,1,0:T(8,128)(2,1)} %get-tuple-element.27), channel_id=1, source_target_pairs={{0,80},{16,64},{32,112},{48,96},{64,144},{80,128},{96,176},{112,16... | collective-permute-start | bytes 491528 | tf_op jit(solution)/shard_map/ppermute | solution.py:79
  98.0 13.1 %collective-permute-start.15 = (bf16[2,2,320,128]{3,2,1,0:T(8,128)(2,1)}, bf16[2,2,320,128]{3,2,1,0:T(8,128)(2,1)S(1)}, u32[]{:S(2)}, u32[]{:S(2)}) collective-permute-start(bf16[2,2,320,128]{3,2,1,0:T(8,128)(2,1)} %get-tuple-element.19), channel_id=1, source_target_pairs={{0,16},{16,0},{32,48},{48,32},{64,80},{80,64},{96,112},{112,96},{1... | collective-permute-start | bytes 983048 | tf_op jit(solution)/shard_map/ppermute | solution.py:79
  103.5 5.6 %copy-start.28 = (bf16[1,2,320,128]{3,2,1,0:T(8,128)(2,1)S(1)}, bf16[1,2,320,128]{3,2,1,0:T(8,128)(2,1)}, u32[]{:S(2)}) copy-start(bf16[1,2,320,128]{3,2,1,0:T(8,128)(2,1)} %get-tuple-element.22) | copy-start | bytes 491524
  103.5 7.1 %copy-start.27 = (bf16[1,2,320,128]{3,2,1,0:T(8,128)(2,1)S(1)}, bf16[1,2,320,128]{3,2,1,0:T(8,128)(2,1)}, u32[]{:S(2)}) copy-start(bf16[1,2,320,128]{3,2,1,0:T(8,128)(2,1)} %get-tuple-element.25) | copy-start | bytes 491524
  103.6 7.6 %copy-start.26 = (bf16[1,2,320,128]{3,2,1,0:T(8,128)(2,1)S(1)}, bf16[1,2,320,128]{3,2,1,0:T(8,128)(2,1)}, u32[]{:S(2)}) copy-start(bf16[1,2,320,128]{3,2,1,0:T(8,128)(2,1)} %get-tuple-element.26) | copy-start | bytes 491524
  104.8 10.5 %collective-permute-start.24 = (bf16[1,2,320,128]{3,2,1,0:T(8,128)(2,1)S(1)}, bf16[1,2,320,128]{3,2,1,0:T(8,128)(2,1)S(1)}, u32[]{:S(2)}, u32[]{:S(2)}) collective-permute-start(bf16[1,2,320,128]{3,2,1,0:T(8,128)(2,1)S(1)} %copy-done.25), channel_id=1, source_target_pairs={{0,48},{16,32},{32,80},{48,64},{64,112},{80,96},{96,144},{112,128}... | collective-permute-start | bytes 491528 | tf_op jit(solution)/shard_map/ppermute | solution.py:79
  106.3 21.2 %copy-start.16 = (bf16[1,2,320,128]{3,2,1,0:T(8,128)(2,1)}, bf16[1,2,320,128]{3,2,1,0:T(8,128)(2,1)S(1)}, u32[]{:S(2)}) copy-start(bf16[1,2,320,128]{3,2,1,0:T(8,128)(2,1)S(1)} %collective-permute-done.19.refs_2_) | copy-start | bytes 491524
  106.4 8.9 %collective-permute-start.17 = (bf16[1,2,320,128]{3,2,1,0:T(8,128)(2,1)S(1)}, bf16[1,2,320,128]{3,2,1,0:T(8,128)(2,1)S(1)}, u32[]{:S(2)}, u32[]{:S(2)}) collective-permute-start(bf16[1,2,320,128]{3,2,1,0:T(8,128)(2,1)S(1)} %copy-done.29), channel_id=1, source_target_pairs={{0,224},{16,240},{32,0},{48,16},{64,32},{80,48},{96,64},{112,80},{... | collective-permute-start | bytes 491528 | tf_op jit(solution)/shard_map/ppermute | solution.py:79
  109.1 18.5 %copy-start.17 = (bf16[1,2,320,128]{3,2,1,0:T(8,128)(2,1)}, bf16[1,2,320,128]{3,2,1,0:T(8,128)(2,1)S(1)}, u32[]{:S(2)}) copy-start(bf16[1,2,320,128]{3,2,1,0:T(8,128)(2,1)S(1)} %collective-permute-done.20.refs_3_) | copy-start | bytes 491524
  109.1 11.1 %collective-permute-start.18 = (bf16[1,2,320,128]{3,2,1,0:T(8,128)(2,1)S(1)}, bf16[1,2,320,128]{3,2,1,0:T(8,128)(2,1)S(1)}, u32[]{:S(2)}, u32[]{:S(2)}) collective-permute-start(bf16[1,2,320,128]{3,2,1,0:T(8,128)(2,1)S(1)} %copy-done.28), channel_id=1, source_target_pairs={{0,192},{16,208},{32,224},{48,240},{64,0},{80,16},{96,32},{112,48}... | collective-permute-start | bytes 491528 | tf_op jit(solution)/shard_map/ppermute | solution.py:79
  110.6 17.0 %copy-start.18 = (bf16[1,2,320,128]{3,2,1,0:T(8,128)(2,1)}, bf16[1,2,320,128]{3,2,1,0:T(8,128)(2,1)S(1)}, u32[]{:S(2)}) copy-start(bf16[1,2,320,128]{3,2,1,0:T(8,128)(2,1)S(1)} %collective-permute-done.23.refs_6_) | copy-start | bytes 491524
  110.6 12.0 %collective-permute-start.21 = (bf16[1,2,320,128]{3,2,1,0:T(8,128)(2,1)S(1)}, bf16[1,2,320,128]{3,2,1,0:T(8,128)(2,1)S(1)}, u32[]{:S(2)}, u32[]{:S(2)}) collective-permute-start(bf16[1,2,320,128]{3,2,1,0:T(8,128)(2,1)S(1)} %copy-done.27), channel_id=1, source_target_pairs={{0,240},{16,224},{32,16},{48,0},{64,48},{80,32},{96,80},{112,64},{... | collective-permute-start | bytes 491528 | tf_op jit(solution)/shard_map/ppermute | solution.py:79
  111.1 15.0 %collective-permute-start.22 = (bf16[1,2,320,128]{3,2,1,0:T(8,128)(2,1)S(1)}, bf16[1,2,320,128]{3,2,1,0:T(8,128)(2,1)S(1)}, u32[]{:S(2)}, u32[]{:S(2)}) collective-permute-start(bf16[1,2,320,128]{3,2,1,0:T(8,128)(2,1)S(1)} %copy-done.26), channel_id=1, source_target_pairs={{0,208},{16,192},{32,240},{48,224},{64,16},{80,0},{96,48},{112,32}... | collective-permute-start | bytes 491528 | tf_op jit(solution)/shard_map/ppermute | solution.py:79
  115.3 12.3 %copy-start.19 = (bf16[1,2,320,128]{3,2,1,0:T(8,128)(2,1)}, bf16[1,2,320,128]{3,2,1,0:T(8,128)(2,1)S(1)}, u32[]{:S(2)}) copy-start(bf16[1,2,320,128]{3,2,1,0:T(8,128)(2,1)S(1)} %collective-permute-done.24.refs_7_) | copy-start | bytes 491524
  115.3 12.3 %copy-start.20 = (bf16[1,2,320,128]{3,2,1,0:T(8,128)(2,1)}, bf16[1,2,320,128]{3,2,1,0:T(8,128)(2,1)S(1)}, u32[]{:S(2)}) copy-start(bf16[1,2,320,128]{3,2,1,0:T(8,128)(2,1)S(1)} %collective-permute-done.17.refs_0_) | copy-start | bytes 491524
  120.2 7.4 %copy-start.21 = (bf16[1,2,320,128]{3,2,1,0:T(8,128)(2,1)}, bf16[1,2,320,128]{3,2,1,0:T(8,128)(2,1)S(1)}, u32[]{:S(2)}) copy-start(bf16[1,2,320,128]{3,2,1,0:T(8,128)(2,1)S(1)} %collective-permute-done.18.refs_1_) | copy-start | bytes 491524
  122.6 5.0 %copy-start.22 = (bf16[1,2,320,128]{3,2,1,0:T(8,128)(2,1)}, bf16[1,2,320,128]{3,2,1,0:T(8,128)(2,1)S(1)}, u32[]{:S(2)}) copy-start(bf16[1,2,320,128]{3,2,1,0:T(8,128)(2,1)S(1)} %collective-permute-done.21.refs_4_) | copy-start | bytes 491524
  (9 other events, 15.9 us)
